TPU v7x, 32 devices: a whole 2x2x4 slice. The times are simulated.
32 devices in a mesh: grp: 2 (over x), ha: 16 (over z, y, core).
Axes of the slice: x: 2, y: 2, z: 4, core: 2. Of those that a mesh axis runs over, the one named last changes fastest.
Arguments:
- features: bfloat16 [4, 16, 128, 384], P('grp', 'ha'), parts along dimension 0, may hold values from -8 to 8
- first_cache: bfloat16 [4, 16, 128, 384], P('grp', 'ha'), parts along dimension 0, may hold values from -6 to 6
- second_cache: bfloat16 [4, 32, 256, 192], P('grp', 'ha'), parts along dimension 0, may hold values from -6 to 6
- w_query: bfloat16 [384, 384], replicated, may hold values from -2 to 2
- w_key: bfloat16 [384, 384], replicated, may hold values from -2 to 2
- w_value: bfloat16 [384, 384], replicated, may hold values from -0.3125 to 0.3125
- w_output: bfloat16 [384, 384], replicated, may hold values from -0.625 to 0.625
- w_first: bfloat16 [3, 3, 3, 384, 384], replicated, may hold values from -0.0625 to 0.0625
- w_upsample: bfloat16 [3, 3, 384, 192], replicated, may hold values from -0.109375 to 0.109375
- w_second: bfloat16 [3, 3, 3, 192, 192], replicated, may hold values from -0.078125 to 0.078125
Outputs:
- decoded: bfloat16 [4, 32, 256, 192], P('grp', 'ha'), parts along dimension 0
There are 2 independent parts, one for each index of `grp`. A program takes and returns all parts, laid end to end along the dimension named above; an argument that names none is the same for every part. Nothing has to cross between parts.
All inputs are finite; a program needn't handle non-finite values.
Results may differ from a plain program's by a relative error of at most 0.015.
Values may be sent and summed in bfloat16 or wider, within the bound.
A program may use at most 128 MiB of HBM per device.

v0:
```python
import math

import jax
import jax.numpy as jnp
from jax import lax
from jax.sharding import PartitionSpec as P


def extended(x, sides, width):
    for axis, dim in sides:
        count, length = (lax.axis_size(axis), x.shape[dim])
        up = [(i, (i + 1) % count) for i in range(count - 1)]
        down = [(j, i) for i, j in up]
        last = lax.slice_in_dim(x, length - width, length, axis=dim)
        first = lax.slice_in_dim(x, 0, width, axis=dim)
        before = lax.ppermute(last, axis, up)
        after = lax.ppermute(first, axis, down)
        x = jnp.concatenate([before, x, after], axis=dim)
    return x


def rms_scale(tensor):
    widened = tensor.astype(jnp.float32)
    return widened * lax.rsqrt(jnp.mean(widened * widened, axis=-1, keepdims=True) + 1e-06)


def conv_taps(padded, weight, time_taps):
    frames_out = padded.shape[0] - time_taps + 1
    height_out = padded.shape[1] - 2
    width_out = padded.shape[2]
    in_channels = weight.shape[-2]
    out_channels = weight.shape[-1]
    widened = jnp.pad(padded, ((0, 0), (0, 0), (1, 1), (0, 0)))
    result = jnp.zeros((frames_out, height_out, width_out, out_channels), jnp.float32)
    for time_off in range(time_taps):
        for row_off in range(3):
            window = widened[time_off : time_off + frames_out, row_off : row_off + height_out]
            stacked = jnp.concatenate(
                [window[:, :, col_off : col_off + width_out] for col_off in range(3)], axis=-1
            )
            kernel = weight[time_off, row_off].reshape(3 * in_channels, out_channels)
            result = result + jnp.einsum(
                "fhwc,cd->fhwd", stacked, kernel, preferred_element_type=jnp.float32
            )
    return result


def project_rows(tokens, weight):
    return jnp.einsum("ftc,cd->ftd", tokens, weight, preferred_element_type=jnp.float32).astype(
        jnp.bfloat16
    )


def per_device(
    features,
    first_cache,
    second_cache,
    w_query,
    w_key,
    w_value,
    w_output,
    w_first,
    w_upsample,
    w_second,
):
    frame_count, row_count, width_count, channels = features.shape
    normed = rms_scale(features).astype(jnp.bfloat16)
    normed_tokens = normed.reshape(frame_count, row_count * width_count, channels)
    queries = project_rows(normed_tokens, w_query)
    score_scale = 1.0 / math.sqrt(channels)
    token_count = row_count * width_count
    keys_own = project_rows(normed_tokens, w_key)
    values_own = project_rows(normed_tokens, w_value)
    running_max = jnp.full((frame_count, token_count), -jnp.inf, jnp.float32)
    weight_sum = jnp.zeros((frame_count, token_count), jnp.float32)
    weighted = jnp.zeros((frame_count, token_count, channels), jnp.float32)
    scores = (
        jnp.einsum(
            "fqc,fkc->fqk",
            queries,
            lax.all_gather(keys_own, "ha", axis=1, tiled=True),
            preferred_element_type=jnp.float32,
        )
        * score_scale
    )
    newest = jnp.max(scores, axis=-1)
    shrink = jnp.exp(running_max - newest)
    weights = jnp.exp(scores - newest[..., None])
    weight_sum = weight_sum * shrink + jnp.sum(weights, axis=-1)
    weighted = weighted * shrink[..., None] + jnp.einsum(
        "fqk,fkc->fqc",
        weights.astype(jnp.bfloat16),
        lax.all_gather(values_own, "ha", axis=1, tiled=True),
        preferred_element_type=jnp.float32,
    )
    running_max, weight_sum, weighted = (newest, weight_sum, weighted)
    attended = (weighted / weight_sum[..., None]).astype(jnp.bfloat16)
    projected = jnp.einsum("ftc,cd->ftd", attended, w_output, preferred_element_type=jnp.float32)
    mixed = (
        features.astype(jnp.float32)
        + projected.reshape(frame_count, row_count, width_count, channels)
    ).astype(jnp.bfloat16)
    first_in = jax.nn.silu(rms_scale(mixed)).astype(jnp.bfloat16)
    first_stack = jnp.concatenate([first_cache, first_in], axis=0)
    first_padded = extended(first_stack, (("ha", 1),), 1)
    block_out = (mixed.astype(jnp.float32) + conv_taps(first_padded, w_first, 3)).astype(
        jnp.bfloat16
    )
    enlarged = jnp.repeat(jnp.repeat(block_out, 2, axis=1), 2, axis=2)
    up_padded = extended(enlarged, (("ha", 1),), 1)
    upsampled = conv_taps(up_padded, w_upsample[None], 1).astype(jnp.bfloat16)
    second_in = jax.nn.silu(rms_scale(upsampled)).astype(jnp.bfloat16)
    second_stack = jnp.concatenate([second_cache, second_in], axis=0)
    second_padded = extended(second_stack, (("ha", 1),), 1)
    return (upsampled.astype(jnp.float32) + conv_taps(second_padded, w_second, 3)).astype(
        jnp.bfloat16
    )


def solution(mesh):
    placed = (
        P("grp", "ha", None, None),
        P("grp", "ha", None, None),
        P("grp", "ha", None, None),
        P(),
        P(),
        P(),
        P(),
        P(),
        P(),
        P(),
    )
    return jax.shard_map(
        per_device,
        mesh=mesh,
        in_specs=placed,
        out_specs=P("grp", "ha", None, None),
        check_vma=False,
    )
```

profile of v0, /device:TPU:1, one launch (start us, length us, event | category | flops | bytes accessed | tf_op | source)
XLA Modules:
  0.0 175.6 jit_solution(18347833795651068395)
XLA Ops:
  6.5 1.1 fusion.144
  7.7 2.1 %convolution_convert_fusion.1 = bf16[2,128,384]{2,1,0:T(8,128)(2,1)} fusion(bf16[384,384]{1,0:T(8,128)(2,1)} %param.14, bf16[2,1,128,384]{3,2,1,0:T(8,128)(2,1)} %param.10, f32[2,128]{1,0:T(2,128)S(1)} %add_rsqrt_fusion.2), kind=kOutput, calls=%fused_computation.121 | convolution fusion | flops 75890688 | bytes 689152 | tf_op jit(solution)/shard_map/ftc,cd->ftd/dot_general | solution.py:49
  9.8 2.1 %convolution_convert_fusion = bf16[2,128,384]{2,1,0:T(8,128)(2,1)} fusion(bf16[384,384]{1,0:T(8,128)(2,1)} %param.15, bf16[2,1,128,384]{3,2,1,0:T(8,128)(2,1)} %param.10, f32[2,128]{1,0:T(2,128)S(1)} %add_rsqrt_fusion.2), kind=kOutput, calls=%fused_computation.120 | convolution fusion | flops 75890688 | bytes 689152 | tf_op jit(solution)/shard_map/ftc,cd->ftd/dot_general | solution.py:49
  11.9 45.7 %all-gather.3.cloned.1.call-done = bf16[2,2048,384]{2,1,0:T(8,128)(2,1)} async-done(((bf16[2,128,384]{2,1,0:T(8,128)(2,1)}), bf16[2,2048,384]{2,1,0:T(8,128)(2,1)}) %all-gather.3.cloned.1.call-update) | async-done | bytes 3145744 | tf_op jit(solution)/shard_map/all_gather | solution.py:81
  57.7 3.3 %fusion.193 = (f32[2,128]{1,0:T(2,128)S(1)}, f32[2,128,2048]{2,1,0:T(8,128)S(1)}) fusion(bf16[2,2048,384]{2,1,0:T(8,128)(2,1)} %all-gather.3.cloned.1.call-done, bf16[384,384]{1,0:T(8,128)(2,1)S(1)} %copy-done, bf16[2,1,128,384]{3,2,1,0:T(8,128)(2,1)S(1)} %copy-done.3, f32[2,128]{1,0:T(2,128)S(1)} %add_rsqrt_fusion.2), kind=kOutput, calls=%fused_computation.238 | convolution fusion | flops 479592192 | bytes 5736448 | tf_op jit(solution)/shard_map/fqc,fkc->fqk/dot_general | solution.py:78
  61.0 0.4 fusion.23
  61.4 42.6 %all-gather.5.cloned.1.call-done = bf16[2,2048,384]{2,1,0:T(8,128)(2,1)} async-done(((bf16[2,128,384]{2,1,0:T(8,128)(2,1)}), bf16[2,2048,384]{2,1,0:T(8,128)(2,1)}) %all-gather.5.cloned.1.call-update) | async-done | bytes 3145744 | tf_op jit(solution)/shard_map/all_gather | solution.py:93
  104.0 3.0 %multiply_reduce_fusion.1 = (f32[2,128]{1,0:T(2,128)S(1)}, f32[2,1,128,384]{3,2,0,1:T(8,128)S(1)}) fusion(bf16[384,384]{1,0:T(8,128)(2,1)S(1)} %copy-done.9, bf16[2,2048,384]{2,1,0:T(8,128)(2,1)} %all-gather.5.cloned.1.call-done, f32[2,128,2048]{2,1,0:T(8,128)S(1)} %get-tuple-element.87, f32[2,128]{1,0:T(2,128)S(1)} %get-tuple-element.86, ...), kind=kOutput, calls=%fused_computation.193 | convolution fusion | flops 480083712 | bytes 6131712 | tf_op jit(solution)/shard_map/ftc,cd->ftd/dot_general | solution.py:98
  107.3 2.3 %collective-permute-start = (bf16[4,1,128,384]{3,2,0,1:T(8,128)(2,1)S(1)}, bf16[4,1,128,384]{3,2,0,1:T(8,128)(2,1)S(1)}, u32[]{:S(2)}, u32[]{:S(2)}) collective-permute-start(bf16[4,1,128,384]{3,2,0,1:T(8,128)(2,1)S(1)} %pad_maximum_fusion.4), channel_id=1, source_target_pairs={{0,1},{1,2},{2,3},{3,4},{4,5},{5,6},{6,7},{7,8},{8,9},{9,10},{10,1... | collective-permute-start | bytes 1179656 | tf_op jit(solution)/shard_map/ppermute | solution.py:16
  109.6 2.0 %collective-permute-start.1 = (bf16[4,1,128,384]{3,2,0,1:T(8,128)(2,1)S(1)}, bf16[4,1,128,384]{3,2,0,1:T(8,128)(2,1)S(1)}, u32[]{:S(2)}, u32[]{:S(2)}) collective-permute-start(bf16[4,1,128,384]{3,2,0,1:T(8,128)(2,1)S(1)} %pad_maximum_fusion.4), channel_id=1, source_target_pairs={{1,0},{2,1},{3,2},{4,3},{5,4},{6,5},{7,6},{8,7},{9,8},{10,9},{11,1... | collective-permute-start | bytes 1179656 | tf_op jit(solution)/shard_map/ppermute | solution.py:17
  111.6 3.9 %fusion.183 = (bf16[1,1,3,384,384]{4,3,2,1,0:T(8,128)(2,1)S(1)}, bf16[1,1,3,384,384]{4,3,2,1,0:T(8,128)(2,1)S(1)}, bf16[1,1,3,384,384]{4,3,2,1,0:T(8,128)(2,1)S(...) fusion(bf16[3,3,3,384,384]{4,3,2,1,0:T(8,128)(2,1)} %param.17), kind=kLoop, calls=%fused_computation.228 | loop fusion | bytes 15925248 | tf_op jit(solution)/shard_map/slice | solution.py:41
  115.6 3.1 %collective-permute-done.1 = bf16[4,1,128,384]{3,2,0,1:T(8,128)(2,1)S(1)} collective-permute-done((bf16[4,1,128,384]{3,2,0,1:T(8,128)(2,1)S(1)}, bf16[4,1,128,384]{3,2,0,1:T(8,128)(2,1)S(1)}, u32[]{:S(2)}, u32[]{:S(2)}) %collective-permute-start.1) | collective-permute-done | bytes 393248 | tf_op jit(solution)/shard_map/ppermute | solution.py:17
  119.0 0.6 fusion.188
  119.7 0.5 fusion.104
  120.2 0.5 convolution_add_fusion.15
  120.7 0.5 convolution_add_fusion.14
  121.2 0.5 convolution_add_fusion.13
  121.7 0.5 convolution_add_fusion.12
  122.2 0.5 convolution_add_fusion.11
  122.7 0.5 convolution_add_fusion.10
  123.2 0.5 convolution_add_fusion.9
  123.7 0.5 copy-done.8
  124.2 0.5 fusion.99
  124.9 0.9 slice.411
  125.8 1.9 %collective-permute-start.2 = (bf16[2,1,256,384]{3,2,1,0:T(8,128)(2,1)}, bf16[2,1,256,384]{3,2,1,0:T(8,128)(2,1)}, u32[]{:S(2)}, u32[]{:S(2)}) collective-permute-start(bf16[2,1,256,384]{3,2,1,0:T(8,128)(2,1)} %slice.411), channel_id=1, source_target_pairs={{0,1},{1,2},{2,3},{3,4},{4,5},{5,6},{6,7},{7,8},{8,9},{9,10},{10,1... | collective-permute-start | bytes 1179656 | tf_op jit(solution)/shard_map/ppermute | solution.py:16
  127.7 3.3 %collective-permute-start.3 = (bf16[2,1,256,384]{3,2,1,0:T(8,128)(2,1)}, bf16[2,1,256,384]{3,2,1,0:T(8,128)(2,1)}, u32[]{:S(2)}, u32[]{:S(2)}) collective-permute-start(bf16[2,1,256,384]{3,2,1,0:T(8,128)(2,1)} %slice.411), channel_id=1, source_target_pairs={{1,0},{2,1},{3,2},{4,3},{5,4},{6,5},{7,6},{8,7},{9,8},{10,9},{11,1... | collective-permute-start | bytes 1179656 | tf_op jit(solution)/shard_map/ppermute | solution.py:17
  131.2 0.4 copy.30
  133.7 5.5 %collective-permute-done.3 = bf16[2,1,256,384]{3,2,1,0:T(8,128)(2,1)} collective-permute-done((bf16[2,1,256,384]{3,2,1,0:T(8,128)(2,1)}, bf16[2,1,256,384]{3,2,1,0:T(8,128)(2,1)}, u32[]{:S(2)}, u32[]{:S(2)}) %collective-permute-start.3) | collective-permute-done | bytes 393248 | tf_op jit(solution)/shard_map/ppermute | solution.py:17
  139.2 1.6 fusion.26
  140.8 0.8 fusion.186
  141.6 1.1 fusion.10
  142.7 1.9 %fusion.18 = f32[2,2,256,192]{2,3,1,0:T(8,128)S(1)} fusion(bf16[2,1,256,384]{3,2,1,0:T(8,128)(2,1)} %collective-permute-done.3, bf16[2,2,256,384]{3,2,1,0:T(8,128)(2,1)S(1)} %broadcast_in_dim.28, bf16[2,2,256,384]{3,2,1,0:T(8,128)(2,1)S(1)} %get-tuple-element.46, bf16[2,2,256,384]{3,2,1,0:T(8,128)(2,1)S(1)} %get-tuple-element.42, ...), kind=kOutput, calls=%fused_computation.28 | convolution fusion | flops 462422016 | bytes 3981312 | tf_op jit(solution)/shard_map/fhwc,cd->fhwd/dot_general | solution.py:42
  144.7 2.0 %multiply_reduce_fusion = (f32[2,2,256]{2,1,0:T(2,128)S(1)}, f32[2,2,256,192]{2,3,1,0:T(8,128)S(1)}) fusion(f32[2,2,256,192]{2,3,1,0:T(8,128)S(1)} %fusion.18, f32[2,2,256,192]{2,3,1,0:T(8,128)S(1)} %fusion.10, bf16[1152,192,1,1]{0,1,2,3:T(8,128)(2,1)S(1)} %reshape.127, bf16[2,2,256,384]{3,2,1,0:T(8,128)(2,1)S(1)} %broadcast_in_dim.28, ...), kind=kOutput, calls=%fused_computation.133 | convolution fusion | flops 463600640 | bytes 5558272 | tf_op jit(solution)/shard_map/fhwc,cd->fhwd/dot_general | solution.py:42
  147.0 2.1 %collective-permute-start.4 = (bf16[4,1,256,192]{2,3,1,0:T(8,128)(2,1)S(1)}, bf16[4,1,256,192]{2,3,1,0:T(8,128)(2,1)S(1)}, u32[]{:S(2)}, u32[]{:S(2)}) collective-permute-start(bf16[4,1,256,192]{2,3,1,0:T(8,128)(2,1)S(1)} %get-tuple-element.76), channel_id=1, source_target_pairs={{0,1},{1,2},{2,3},{3,4},{4,5},{5,6},{6,7},{7,8},{8,9},{9,10},{10,1... | collective-permute-start | bytes 1179656 | tf_op jit(solution)/shard_map/ppermute | solution.py:16
  149.1 2.6 %collective-permute-start.5 = (bf16[4,1,256,192]{2,3,1,0:T(8,128)(2,1)S(1)}, bf16[4,1,256,192]{2,3,1,0:T(8,128)(2,1)S(1)}, u32[]{:S(2)}, u32[]{:S(2)}) collective-permute-start(bf16[4,1,256,192]{2,3,1,0:T(8,128)(2,1)S(1)} %get-tuple-element.77), channel_id=1, source_target_pairs={{1,0},{2,1},{3,2},{4,3},{5,4},{6,5},{7,6},{8,7},{9,8},{10,9},{11,1... | collective-permute-start | bytes 1179656 | tf_op jit(solution)/shard_map/ppermute | solution.py:17
  152.0 1.8 %collective-permute-done.4 = bf16[4,1,256,192]{2,3,1,0:T(8,128)(2,1)S(1)} collective-permute-done((bf16[4,1,256,192]{2,3,1,0:T(8,128)(2,1)S(1)}, bf16[4,1,256,192]{2,3,1,0:T(8,128)(2,1)S(1)}, u32[]{:S(2)}, u32[]{:S(2)}) %collective-permute-start.4) | collective-permute-done | bytes 393248 | tf_op jit(solution)/shard_map/ppermute | solution.py:16
  153.8 5.3 %collective-permute-done.5 = bf16[4,1,256,192]{2,3,1,0:T(8,128)(2,1)S(1)} collective-permute-done((bf16[4,1,256,192]{2,3,1,0:T(8,128)(2,1)S(1)}, bf16[4,1,256,192]{2,3,1,0:T(8,128)(2,1)S(1)}, u32[]{:S(2)}, u32[]{:S(2)}) %collective-permute-start.5) | collective-permute-done | bytes 393248 | tf_op jit(solution)/shard_map/ppermute | solution.py:17
  159.1 2.0 %select_maximum_fusion = bf16[4,4,258,192]{2,3,1,0:T(8,128)(2,1)S(1)} fusion(bf16[4,1,256,192]{2,3,1,0:T(8,128)(2,1)S(1)} %collective-permute-done.5, bf16[4,1,256,192]{2,3,1,0:T(8,128)(2,1)S(1)} %collective-permute-done.4, bf16[2,2,256,192]{2,3,1,0:T(8,128)(2,1)S(1)} %multiply_convert_fusion, bf16[2,2,256,192]{2,3,1,0:T(8,128)(2,1)S(1)} %copy-done.2), kind=kLoop, calls=%fused_computation.10 | loop fusion | flops 11888640 | bytes 3158016 | tf_op jit(solution)/shard_map/concatenate | solution.py:18
  161.1 1.7 fusion.185
  163.2 0.5 fusion.57
  163.8 0.5 convolution_add_fusion.7
  164.3 0.5 convolution_add_fusion.6
  164.8 0.5 convolution_add_fusion.5
  165.3 0.5 convolution_add_fusion.4
  165.9 0.5 convolution_add_fusion.3
  166.4 0.5 convolution_add_fusion.2
  166.9 0.5 convolution_add_fusion.1
  167.4 1.3 fusion.43
  (49 shorter events, 4.2 us)
Async XLA Ops:
  6.5 51.1 %copy-start = (bf16[384,384]{1,0:T(8,128)(2,1)S(1)}, bf16[384,384]{1,0:T(8,128)(2,1)}, u32[]{:S(2)}) copy-start(bf16[384,384]{1,0:T(8,128)(2,1)} %param.13) | copy-start | bytes 884740
  6.5 51.1 %copy-start.3 = (bf16[2,1,128,384]{3,2,1,0:T(8,128)(2,1)S(1)}, bf16[2,1,128,384]{3,2,1,0:T(8,128)(2,1)}, u32[]{:S(2)}) copy-start(bf16[2,1,128,384]{3,2,1,0:T(8,128)(2,1)} %param.10) | copy-start | bytes 589828
  6.5 51.1 %all-gather.3.cloned.1.call-start = ((), (), s32[]{:S(2)}) async-start(), calls=%async_computation | async-start | bytes 3342336 | tf_op jit(solution)/shard_map/all_gather | solution.py:81
  9.8 94.2 %all-gather.5.cloned.1.call-start = ((), (), s32[]{:S(2)}) async-start(), calls=%async_computation.1 | async-start | bytes 3342336 | tf_op jit(solution)/shard_map/all_gather | solution.py:93
  60.9 43.1 %copy-start.9 = (bf16[384,384]{1,0:T(8,128)(2,1)S(1)}, bf16[384,384]{1,0:T(8,128)(2,1)}, u32[]{:S(2)}) copy-start(bf16[384,384]{1,0:T(8,128)(2,1)} %param.16) | copy-start | bytes 884740
  104.0 3.2 %copy-start.5 = (bf16[2,1,128,384]{3,2,1,0:T(8,128)(2,1)S(1)}, bf16[2,1,128,384]{3,2,1,0:T(8,128)(2,1)}, u32[]{:S(2)}) copy-start(bf16[2,1,128,384]{3,2,1,0:T(8,128)(2,1)} %param.11) | copy-start | bytes 589828
  107.0 8.6 %copy-start.7 = (f32[2,1,128,384]{3,2,0,1:T(8,128)}, f32[2,1,128,384]{3,2,0,1:T(8,128)S(1)}, u32[]{:S(2)}) copy-start(f32[2,1,128,384]{3,2,0,1:T(8,128)S(1)} %get-tuple-element.89) | copy-start | bytes 1179652
  107.3 8.4 %collective-permute-start = (bf16[4,1,128,384]{3,2,0,1:T(8,128)(2,1)S(1)}, bf16[4,1,128,384]{3,2,0,1:T(8,128)(2,1)S(1)}, u32[]{:S(2)}, u32[]{:S(2)}) collective-permute-start(bf16[4,1,128,384]{3,2,0,1:T(8,128)(2,1)S(1)} %pad_maximum_fusion.4), channel_id=1, source_target_pairs={{0,1},{1,2},{2,3},{3,4},{4,5},{5,6},{6,7},{7,8},{8,9},{9,10},{10,1... | collective-permute-start | bytes 1179656 | tf_op jit(solution)/shard_map/ppermute | solution.py:16
  109.6 9.1 %collective-permute-start.1 = (bf16[4,1,128,384]{3,2,0,1:T(8,128)(2,1)S(1)}, bf16[4,1,128,384]{3,2,0,1:T(8,128)(2,1)S(1)}, u32[]{:S(2)}, u32[]{:S(2)}) collective-permute-start(bf16[4,1,128,384]{3,2,0,1:T(8,128)(2,1)S(1)} %pad_maximum_fusion.4), channel_id=1, source_target_pairs={{1,0},{2,1},{3,2},{4,3},{5,4},{6,5},{7,6},{8,7},{9,8},{10,9},{11,1... | collective-permute-start | bytes 1179656 | tf_op jit(solution)/shard_map/ppermute | solution.py:17
  123.2 1.0 copy-start.8
  124.2 6.9 %copy-start.6 = (bf16[3,3,384,192]{2,3,1,0:T(8,128)(2,1)S(1)}, bf16[3,3,384,192]{2,3,1,0:T(8,128)(2,1)}, u32[]{:S(2)}) copy-start(bf16[3,3,384,192]{2,3,1,0:T(8,128)(2,1)} %param.18) | copy-start | bytes 3981316
  125.8 7.9 %collective-permute-start.2 = (bf16[2,1,256,384]{3,2,1,0:T(8,128)(2,1)}, bf16[2,1,256,384]{3,2,1,0:T(8,128)(2,1)}, u32[]{:S(2)}, u32[]{:S(2)}) collective-permute-start(bf16[2,1,256,384]{3,2,1,0:T(8,128)(2,1)} %slice.411), channel_id=1, source_target_pairs={{0,1},{1,2},{2,3},{3,4},{4,5},{5,6},{6,7},{7,8},{8,9},{9,10},{10,1... | collective-permute-start | bytes 1179656 | tf_op jit(solution)/shard_map/ppermute | solution.py:16
  127.7 11.5 %collective-permute-start.3 = (bf16[2,1,256,384]{3,2,1,0:T(8,128)(2,1)}, bf16[2,1,256,384]{3,2,1,0:T(8,128)(2,1)}, u32[]{:S(2)}, u32[]{:S(2)}) collective-permute-start(bf16[2,1,256,384]{3,2,1,0:T(8,128)(2,1)} %slice.411), channel_id=1, source_target_pairs={{1,0},{2,1},{3,2},{4,3},{5,4},{6,5},{7,6},{8,7},{9,8},{10,9},{11,1... | collective-permute-start | bytes 1179656 | tf_op jit(solution)/shard_map/ppermute | solution.py:17
  144.7 2.3 %copy-start.2 = (bf16[2,2,256,192]{2,3,1,0:T(8,128)(2,1)S(1)}, bf16[2,2,256,192]{2,3,1,0:T(8,128)(2,1)}, u32[]{:S(2)}) copy-start(bf16[2,2,256,192]{2,3,1,0:T(8,128)(2,1)} %param.12) | copy-start | bytes 1179652
  146.7 5.1 %copy-start.4 = (bf16[3,3,3,192,192]{4,3,2,1,0:T(8,128)(2,1)S(1)}, bf16[3,3,3,192,192]{4,3,2,1,0:T(8,128)(2,1)}, u32[]{:S(2)}) copy-start(bf16[3,3,3,192,192]{4,3,2,1,0:T(8,128)(2,1)} %param.19) | copy-start | bytes 5971972
  147.0 6.8 %collective-permute-start.4 = (bf16[4,1,256,192]{2,3,1,0:T(8,128)(2,1)S(1)}, bf16[4,1,256,192]{2,3,1,0:T(8,128)(2,1)S(1)}, u32[]{:S(2)}, u32[]{:S(2)}) collective-permute-start(bf16[4,1,256,192]{2,3,1,0:T(8,128)(2,1)S(1)} %get-tuple-element.76), channel_id=1, source_target_pairs={{0,1},{1,2},{2,3},{3,4},{4,5},{5,6},{6,7},{7,8},{8,9},{9,10},{10,1... | collective-permute-start | bytes 1179656 | tf_op jit(solution)/shard_map/ppermute | solution.py:16
  149.1 10.0 %collective-permute-start.5 = (bf16[4,1,256,192]{2,3,1,0:T(8,128)(2,1)S(1)}, bf16[4,1,256,192]{2,3,1,0:T(8,128)(2,1)S(1)}, u32[]{:S(2)}, u32[]{:S(2)}) collective-permute-start(bf16[4,1,256,192]{2,3,1,0:T(8,128)(2,1)S(1)} %get-tuple-element.77), channel_id=1, source_target_pairs={{1,0},{2,1},{3,2},{4,3},{5,4},{6,5},{7,6},{8,7},{9,8},{10,9},{11,1... | collective-permute-start | bytes 1179656 | tf_op jit(solution)/shard_map/ppermute | solution.py:17
  167.4 1.3 copy-start.1
Sparse Core Ops, SparseCore 0:
  9.9 47.7 all-gather.2
  59.9 44.0 all-gather.4
where the time goes:
time: 178 us; the launch traced here: 176 us
  waiting for transfers between devices  104 us (58%)
  matrix products  25.3 us (14%)
  starting transfers between devices  14.3 us (8%)
  between operations  13.9 us (8%)
  local copies, waits for them, and re-layouts  11.8 us (7%)
  other arithmetic  6.13 us (3%)
    all_gather x1, waiting for transfers between devices, per_device(): lax.all_gather(keys_own, 'ha', axis=1, tiled=True)  45.7 us
    all_gather x1, waiting for transfers between devices, per_device(): lax.all_gather(values_own, 'ha', axis=1, tiled=True)  42.6 us
    dot_general x21, matrix products, conv_taps(): jnp.einsum('fhwc,cd->fhwd', stacked, kernel, preferred_element_type=jnp.f...  14.9 us
    ppermute x3, waiting for transfers between devices, extended(): after = lax.ppermute(first, axis, down)  13.9 us
    ppermute x3, starting transfers between devices, extended(): after = lax.ppermute(first, axis, down)  7.99 us
    ppermute x3, starting transfers between devices, extended(): before = lax.ppermute(last, axis, up)  6.29 us
    slice x6, local copies, waits for them, and re-layouts, conv_taps(): kernel = weight[time_off, row_off].reshape(3 * in_channels, out_channels)  5.42 us
    dot_general x2, matrix products, project_rows(): jnp.einsum('ftc,cd->ftd', tokens, weight, preferred_element_type=jnp.floa...  4.17 us
  transfers between devices with their start and end apart: 8, of which 6 were waited for; matrix products, arithmetic and copies ran while one was open for 7% of the time, Pallas kernels for 0%

commit v1 on v0

v1 whole, which is shorter than its diff:
```python
import functools
import math

import jax
import jax.numpy as jnp
from jax import lax
from jax.experimental import pallas as pl
from jax.experimental.pallas import tpu as pltpu
from jax.sharding import PartitionSpec as P

F32 = jnp.float32
BF16 = jnp.bfloat16


def dot(a, b):
    return jnp.dot(a, b, preferred_element_type=F32)


def dot_t(a, b):
    return lax.dot_general(a, b, (((1,), (1,)), ((), ())), preferred_element_type=F32)


def rms(v):
    return v * lax.rsqrt(jnp.mean(v * v, axis=-1, keepdims=True) + 1e-06)


def silu(v):
    return v / (1.0 + jnp.exp(-v))


def from_left(v, width):
    at = lax.broadcasted_iota(jnp.int32, v.shape, 0) % width
    return jnp.where(at == 0, 0.0, pltpu.roll(v, 1, 0))


def from_right(v, width):
    at = lax.broadcasted_iota(jnp.int32, v.shape, 0) % width
    return jnp.where(at == width - 1, 0.0, pltpu.roll(v, v.shape[0] - 1, 0))


def kernel(
    n,
    feat, fc, sc, wq, wk, wv, wo, w1_hbm, wu_hbm, w2_hbm,
    out,
    fb, ring, acc, top, total, fs, mx, bo, ss, up, c1, c2, w1, wu, w2,
    l_sem, e0_s, e0_r, g_s, g_r, h_s, h_r, e1_s, e1_r, e2_s, e2_r,
):
    width, chan = feat.shape[1], feat.shape[2]
    chan2 = w2.shape[-1]
    chips = n // 2
    half = chips // 2
    me = lax.axis_index("ha")
    core, chip = me % 2, me // 2
    other = 1 - core
    zz, yy = chip // 2, chip % 2
    place = zz + yy * (2 * half - 1 - 2 * zz)

    def at_place(p):
        side = p // half
        level = p + side * (2 * half - 1 - 2 * p)
        return (level * 2 + side) * 2 + core

    nxt = at_place((place + 1) % chips)
    prv = at_place((place + chips - 1) % chips)
    partner = chip * 2 + other
    first, last = me == 0, me == n - 1
    low, high = chip > 0, chip < chips - 1

    def copy(src, dst, ssem, rsem, dev):
        return pltpu.make_async_remote_copy(
            src_ref=src, dst_ref=dst, send_sem=ssem, recv_sem=rsem,
            device_id={"ha": dev}, device_id_type=pl.DeviceIdType.MESH,
        )

    loads = [
        pltpu.make_async_copy(src, dst, l_sem.at[k])
        for k, (src, dst) in enumerate(((w1_hbm, w1), (w2_hbm, w2), (wu_hbm, wu)))
    ]
    for load in loads:
        load.start()

    barrier = pltpu.get_barrier_semaphore()

    def greet(dev):
        pl.semaphore_signal(
            barrier, inc=1, device_id={"ha": dev}, device_id_type=pl.DeviceIdType.MESH
        )

    greet(partner)
    greet(nxt)
    greet(prv)

    @pl.when(jnp.logical_and(core == 0, low))
    def _():
        greet(2 * chip - 2)
        greet(2 * chip - 1)

    @pl.when(jnp.logical_and(core == 1, high))
    def _():
        greet(2 * chip + 2)
        greet(2 * chip + 3)

    pl.semaphore_wait(barrier, 3 + low.astype(jnp.int32) + high.astype(jnp.int32))

    swap = copy(feat.at[other], fb.at[core], e0_s.at[0], e0_r.at[0], partner)
    swap.start()

    def ring_copy(src_slot, slot, row, dev):
        return copy(
            ring.at[src_slot, row], ring.at[slot, row], g_s.at[slot, row], g_r.at[slot, row], dev
        )

    fb[core] = feat[core]
    ring[0, core] = rms(feat[core].astype(F32)).astype(BF16)
    ring_copy(0, 1, core, nxt).start()
    ring_copy(0, chips - 1, core, prv).start()
    copy(feat.at[core], fb.at[other], e0_s.at[0], e0_r.at[0], partner).wait_recv()
    ring[0, other] = rms(fb[other].astype(F32)).astype(BF16)
    ring_copy(0, 1, other, nxt).start()
    ring_copy(0, chips - 1, other, prv).start()

    fc_up = copy(fc, fs.at[pl.ds(0, 2), 0], h_s.at[0], h_r.at[0], me + 1)
    fc_down = copy(fc, fs.at[pl.ds(0, 2), 2], h_s.at[1], h_r.at[1], me - 1)
    sc_up = copy(sc.at[1], ss.at[0, :, pl.ds(0, 2)], h_s.at[2], h_r.at[2], me + 1)
    sc_down = copy(sc.at[0], ss.at[3, :, pl.ds(0, 2)], h_s.at[3], h_r.at[3], me - 1)

    @pl.when(jnp.logical_not(last))
    def _():
        fc_up.start()
        sc_up.start()

    @pl.when(jnp.logical_not(first))
    def _():
        fc_down.start()
        sc_down.start()

    fs[0:2, 1] = fc[...]
    ss[1, :, 0:2] = sc[0]
    ss[2, :, 0:2] = sc[1]

    @pl.when(first)
    def _():
        fs[:, 0] = jnp.zeros((4, width, chan), BF16)
        ss[0, :, 0:2] = jnp.zeros((2, 2, width, chan2), BF16)
        bo[0] = jnp.zeros((2, width, chan), BF16)

    @pl.when(last)
    def _():
        fs[:, 2] = jnp.zeros((4, width, chan), BF16)
        ss[3, :, 0:2] = jnp.zeros((2, 2, width, chan2), BF16)
        bo[2] = jnp.zeros((2, width, chan), BF16)

    own = ring[0].reshape(2 * width, chan)
    queries = dot(own, wq[...]).astype(BF16)
    queries = (dot_t(queries, wk[...]) * (1.0 / math.sqrt(chan))).astype(BF16)

    def scores_of(slot):
        return dot_t(queries, ring[slot].reshape(2 * width, chan))

    scores = scores_of(0)
    largest = jnp.max(scores, axis=-1, keepdims=True)
    weights = jnp.exp(scores - largest)
    top[...] = largest
    total[...] = jnp.sum(weights, axis=-1, keepdims=True)
    acc[...] = dot(weights.astype(BF16), own)

    def attend(slots):
        parts = [scores_of(slot) for slot in slots]
        before = top[...]
        largest = before
        for part in parts:
            largest = jnp.maximum(largest, jnp.max(part, axis=-1, keepdims=True))
        shrink = jnp.exp(before - largest)
        sums, mixed_in = total[...] * shrink, acc[...] * shrink
        for slot, part in zip(slots, parts):
            weights = jnp.exp(part - largest)
            sums += jnp.sum(weights, axis=-1, keepdims=True)
            mixed_in += dot(weights.astype(BF16), ring[slot].reshape(2 * width, chan))
        top[...] = largest
        total[...] = sums
        acc[...] = mixed_in

    for step in range(1, half):
        for row in (core, other):
            ring_copy(step, step, row, nxt).wait_recv()
            if step + 1 < half:
                ring_copy(step, step + 1, row, nxt).start()
            else:
                pl.when(row == 0)(ring_copy(step, step + 1, 0, nxt).start)
            ring_copy(chips - step, chips - step, row, prv).wait_recv()
            if step + 1 < half:
                ring_copy(chips - step, chips - step - 1, row, prv).start()
            else:
                pl.when(row == 1)(ring_copy(chips - step, chips - step - 1, 1, prv).start)
        attend((step, chips - step))

    @pl.when(jnp.logical_not(first))
    def _():
        fc_up.wait_recv()
        sc_up.wait_recv()

    @pl.when(jnp.logical_not(last))
    def _():
        fc_down.wait_recv()
        sc_down.wait_recv()

    for load in loads:
        load.wait()

    def first_conv(times):
        totals = [None] * 3
        for a in times:
            for b in range(3):
                rows = fs[a : a + 2, b].reshape(2 * width, chan)
                for c in range(3):
                    term = dot(rows, w1[a, b, c])
                    totals[c] = term if totals[c] is None else totals[c] + term
        return totals

    def second_conv(times, k):
        taps = (((0, 1), (1, 2)), ((0, 0), (1, 1)), ((1, 0),), ((0, 2),))[k]
        sums = None
        for a in times:
            for b in range(3):
                for parity, c in taps:
                    rows = ss[b : b + 2, parity, a : a + 2].reshape(4 * width, chan2)
                    term = dot(rows, w2[a, b, c])
                    sums = term if sums is None else sums + term
        return sums

    for c, part in enumerate(first_conv((0,))):
        c1[c] = part
    for k in range(4):
        c2[k] = second_conv((0,), k)

    ring_copy(half, half, 0, nxt).wait_recv()
    ring_copy(half, half, 1, prv).wait_recv()
    attend((half,))

    attended = dot((acc[...] / total[...]).astype(BF16), wv[...])
    projected = dot(attended.astype(BF16), wo[...])
    mixed = (fb[...].reshape(2 * width, chan).astype(F32) + projected).astype(BF16)
    entering = silu(rms(mixed.astype(F32))).astype(BF16).reshape(2, width, chan)
    mixed = mixed.reshape(2, width, chan)
    mine = 2 + core
    fs[mine, pl.ds(other, 2)] = entering
    mx[0] = mixed[0]
    mx[1] = mixed[1]

    to_partner = copy(
        fs.at[mine, pl.ds(other, 2)], fs.at[mine, pl.ds(core, 2)], e1_s.at[0], e1_r.at[0], partner
    )
    mix_partner = copy(mx.at[other], mx.at[2], e1_s.at[1], e1_r.at[1], partner)
    row_up = copy(
        fs.at[mine, other + 1], fs.at[mine, 0], e1_s.at[2], e1_r.at[2 + core], 2 * chip + 2
    )
    row_down = copy(
        fs.at[mine, other], fs.at[mine, 2], e1_s.at[3], e1_r.at[2 + core], 2 * chip - 1
    )
    pl.when(high)(row_up.start)
    pl.when(low)(row_down.start)
    to_partner.start()
    mix_partner.start()

    theirs = 2 + other
    copy(
        fs.at[theirs, pl.ds(core, 2)], fs.at[theirs, pl.ds(other, 2)],
        e1_s.at[0], e1_r.at[0], partner,
    ).wait_recv()
    mix_partner.wait_recv()

    @pl.when(jnp.logical_and(core == 0, low))
    def _():
        for f in range(2):
            copy(
                fs.at[2 + f, 1], fs.at[2 + f, 0], e1_s.at[2], e1_r.at[2 + f], 2 * chip - 2 + f
            ).wait_recv()

    @pl.when(jnp.logical_and(core == 1, high))
    def _():
        for f in range(2):
            copy(
                fs.at[2 + f, 1], fs.at[2 + f, 2], e1_s.at[3], e1_r.at[2 + f], 2 * chip + 2 + f
            ).wait_recv()

    sums = [c1[c] + part for c, part in enumerate(first_conv((1, 2)))]
    block = from_left(sums[0], width) + sums[1] + from_right(sums[2], width)
    block = block.reshape(2, width, chan)
    bo[1, core] = (mx[core].astype(F32) + jnp.where(core == 0, block[0], block[1])).astype(BF16)
    bo[1, other] = (mx[2].astype(F32) + jnp.where(core == 0, block[1], block[0])).astype(BF16)

    bo_up = copy(bo.at[1], bo.at[0], e2_s.at[0], e2_r.at[0], me + 1)
    bo_down = copy(bo.at[1], bo.at[2], e2_s.at[1], e2_r.at[1], me - 1)
    pl.when(jnp.logical_not(last))(bo_up.start)
    pl.when(jnp.logical_not(first))(bo_down.start)

    here = bo[1].reshape(2 * width, chan)
    y = [[dot(here, wu[b, c]) for c in range(3)] for b in range(3)]
    rows = [
        [y[2][c] for c in range(3)],
        [y[1][c] + y[2][c] for c in range(3)],
        [y[0][c] + y[1][c] for c in range(3)],
        [y[0][c] for c in range(3)],
    ]
    pl.when(jnp.logical_not(first))(bo_up.wait_recv)
    pl.when(jnp.logical_not(last))(bo_down.wait_recv)
    above = bo[0].reshape(2 * width, chan)
    below = bo[2].reshape(2 * width, chan)
    for c in range(3):
        near, far = dot(above, wu[0, c]), dot(above, wu[1, c])
        rows[0][c] += near + far
        rows[1][c] += near
        near, far = dot(below, wu[2, c]), dot(below, wu[1, c])
        rows[2][c] += near
        rows[3][c] += near + far
    for u in range(4):
        left, middle, right = rows[u]
        phases = (
            from_left(left, width) + middle + right,
            left + middle + from_right(right, width),
        )
        for parity, value in enumerate(phases):
            value = value.astype(BF16)
            if u in (1, 2):
                up[u - 1, parity] = value.reshape(2, width, chan2)
            entering = silu(rms(value.astype(F32)))
            if u == 0:
                entering = jnp.where(first, 0.0, entering)
            if u == 3:
                entering = jnp.where(last, 0.0, entering)
            ss[u, parity, 2:4] = entering.astype(BF16).reshape(2, width, chan2)

    late = (1, 2)
    even = c2[0] + second_conv(late, 0) + from_left(c2[2] + second_conv(late, 2), width)
    out[:, 0] = (up[:, 0].astype(F32) + even.reshape(2, 2, width, chan2)).astype(BF16)
    odd = c2[1] + second_conv(late, 1) + from_right(c2[3] + second_conv(late, 3), width)
    out[:, 1] = (up[:, 1].astype(F32) + odd.reshape(2, 2, width, chan2)).astype(BF16)

    swap.wait_send()
    for slot in range(1, chips):
        for row in range(2):
            ring_copy(slot, slot, row, nxt).wait_send()

    @pl.when(jnp.logical_not(last))
    def _():
        fc_up.wait_send()
        sc_up.wait_send()
        bo_up.wait_send()

    @pl.when(jnp.logical_not(first))
    def _():
        fc_down.wait_send()
        sc_down.wait_send()
        bo_down.wait_send()

    pl.when(high)(row_up.wait_send)
    pl.when(low)(row_down.wait_send)
    to_partner.wait_send()
    mix_partner.wait_send()


def per_device(features, first_cache, second_cache, wq, wk, wv, wo, w1, wu, w2):
    n = lax.axis_size("ha")
    width, chan = features.shape[2:]
    chan2 = w2.shape[-1]
    chips = n // 2
    feat = features.reshape(2, width, chan)
    fc = first_cache.reshape(2, width, chan)
    sc = second_cache.reshape(2, 2, width, 2, chan2).transpose(1, 3, 0, 2, 4)
    vmem = pl.BlockSpec(memory_space=pltpu.VMEM)
    hbm = pl.BlockSpec(memory_space=pl.ANY)
    dma = pltpu.SemaphoreType.DMA
    out = pl.pallas_call(
        functools.partial(kernel, n),
        out_shape=jax.ShapeDtypeStruct((2, 2, 2, width, chan2), BF16),
        in_specs=[vmem] * 7 + [hbm] * 3,
        out_specs=vmem,
        scratch_shapes=[
            pltpu.VMEM((2, width, chan), BF16),
            pltpu.VMEM((chips, 2, width, chan), BF16),
            pltpu.VMEM((2 * width, chan), F32),
            pltpu.VMEM((2 * width, 1), F32),
            pltpu.VMEM((2 * width, 1), F32),
            pltpu.VMEM((4, 3, width, chan), BF16),
            pltpu.VMEM((3, width, chan), BF16),
            pltpu.VMEM((3, 2, width, chan), BF16),
            pltpu.VMEM((4, 2, 4, width, chan2), BF16),
            pltpu.VMEM((2, 2, 2, width, chan2), BF16),
            pltpu.VMEM((3, 2 * width, chan), F32),
            pltpu.VMEM((4, 4 * width, chan2), F32),
            pltpu.VMEM(w1.shape, BF16),
            pltpu.VMEM(wu.shape, BF16),
            pltpu.VMEM(w2.shape, BF16),
            dma((3,)),
            dma((1,)),
            dma((1,)),
            dma((chips, 2)),
            dma((chips, 2)),
            dma((4,)),
            dma((4,)),
            dma((4,)),
            dma((4,)),
            dma((2,)),
            dma((2,)),
        ],
        compiler_params=pltpu.CompilerParams(
            collective_id=0, has_side_effects=True, vmem_limit_bytes=56 * 2**20
        ),
        name="decoder_window",
    )(feat, fc, sc, wq, wk, wv, wo, w1, wu, w2)
    return out.transpose(2, 0, 3, 1, 4).reshape(2, 2, 2 * width, chan2)


def solution(mesh):
    split = P("grp", "ha", None, None)
    return jax.shard_map(
        per_device,
        mesh=mesh,
        in_specs=(split,) * 3 + (P(),) * 7,
        out_specs=split,
        check_vma=False,
    )
```

time: 178 us -> 60.1 us (0.34)
  the two profiles are of different devices: /device:TPU:1 before, /device:TPU:9 now
where the time goes in v1:
time: 60.1 us; the launch traced here: 59.9 us
  Pallas kernels  52.7 us (88%)
  local copies, waits for them, and re-layouts  7.2 us (12%)
    pallas_call x1, Pallas kernels, per_device(): pl.pallas_call(functools.partial(kernel, n), out_shape=jax.ShapeDtypeStru...  52.7 us
    unnamed x4, local copies, waits for them, and re-layouts  3.67 us
    transpose x1, local copies, waits for them, and re-layouts, per_device(): return out.transpose(2, 0, 3, 1, 4).reshape(2, 2, 2 * width, chan2)  1.58 us

profile of v1, /device:TPU:9, one launch (start us, length us, event | category | flops | bytes accessed | tf_op | source)
XLA Modules:
  0.0 59.9 jit_solution(9312262210321110817)
XLA Ops:
  0.0 0.0 copy-start
  0.0 1.4 %copy.12 = bf16[2,2,256,192]{3,1,2,0:T(2,128)(2,1)S(1)} copy(bf16[2,2,256,192]{2,3,1,0:T(8,128)(2,1)} %param.12) | data formatting | bytes 786432 | tf_op args[2]
  1.4 0.9 %copy.18 = bf16[2,2,128,2,192]{4,2,0,3,1:T(8,128)(2,1)} copy(bf16[2,2,128,2,192]{4,1,3,2,0:T(2,128)(2,1)S(1)} %bitcast.11) | data formatting | bytes 786432 | tf_op jit(solution)/shard_map/reshape | solution.py:369
  2.3 0.0 copy-done
  2.3 2.2 %copy.14.wu_hbm = bf16[3,3,384,192]{3,2,1,0:T(8,128)(2,1)} copy(bf16[3,3,384,192]{2,3,1,0:T(8,128)(2,1)S(1)} %copy-done) | data formatting | bytes 2654208 | tf_op args[8]
  4.6 52.7 %decoder_window.1 = bf16[2,2,2,128,192]{4,3,2,1,0:T(8,128)(2,1)} custom-call(bf16[2,128,384]{2,1,0:T(8,128)(2,1)} %bitcast.12, bf16[2,128,384]{2,1,0:T(8,128)(2,1)} %bitcast.13, bf16[2,2,2,128,192]{4,3,2,1,0:T(8,128)(2,1)} %bitcast.8, bf16[384,384]{1,0:T(8,128)(2,1)} %wq.1, bf16[384,384]{1,0:T(8,128)(2,1)} %wk.1, bf16[384,384]{1,0:T(8,128)(2,1)} %wv.1, ...), custom_call_target="tpu_custom_call" | custom-call | tf_op jit(solution)/shard_map/decoder_window/pallas_call | solution.py:373
  57.2 1.6 %copy.15 = bf16[2,2,128,2,192]{4,1,3,2,0:T(2,128)(2,1)S(1)} copy(bf16[2,2,128,2,192]{4,2,0,3,1:T(8,128)(2,1)} %bitcast.9) | data formatting | bytes 786432 | tf_op jit(solution)/shard_map/transpose | solution.py:411
  58.8 1.1 %copy.16 = bf16[2,2,256,192]{2,3,1,0:T(8,128)(2,1)} copy(bf16[2,2,256,192]{3,1,2,0:T(2,128)(2,1)S(1)} %bitcast.10) | data formatting | bytes 786432 | tf_op jit(solution)/shard_map/reshape | solution.py:411
Async XLA Ops:
  0.0 2.3 %copy-start = (bf16[3,3,384,192]{2,3,1,0:T(8,128)(2,1)S(1)}, bf16[3,3,384,192]{2,3,1,0:T(8,128)(2,1)}, u32[]{:S(2)}) copy-start(bf16[3,3,384,192]{2,3,1,0:T(8,128)(2,1)} %param.18) | copy-start | bytes 3981316

commit v2 on v1

--- a/solution.py
+++ b/solution.py
@@ -25,7 +25,7 @@
 
 
 def silu(v):
-    return v / (1.0 + jnp.exp(-v))
+    return v * (0.5 + 0.5 * jnp.tanh(0.5 * v))
 
 
 def from_left(v, width):
@@ -40,9 +40,10 @@
 
 def kernel(
     n,
-    feat, fc, sc, wq, wk, wv, wo, w1_hbm, wu_hbm, w2_hbm,
+    feat, fc, sc, wq_hbm, wk_hbm, wv_hbm, wo_hbm, w1_hbm, wu_hbm, w2_hbm,
     out,
-    fb, ring, acc, top, total, fs, mx, bo, ss, up, c1, c2, w1, wu, w2,
+    fb, ring, acc, top, total, fs, mx, bo, ss, up, c1, c2,
+    wq, wk, wv, wo, w1, wu, w2, wu_turned,
     l_sem, e0_s, e0_r, g_s, g_r, h_s, h_r, e1_s, e1_r, e2_s, e2_r,
 ):
     width, chan = feat.shape[1], feat.shape[2]
@@ -74,10 +75,13 @@
 
     loads = [
         pltpu.make_async_copy(src, dst, l_sem.at[k])
-        for k, (src, dst) in enumerate(((w1_hbm, w1), (w2_hbm, w2), (wu_hbm, wu)))
+        for k, (src, dst) in enumerate(
+            (
+                (wq_hbm, wq), (wk_hbm, wk), (wu_hbm, wu_turned), (w1_hbm, w1),
+                (w2_hbm, w2), (wv_hbm, wv), (wo_hbm, wo),
+            )
+        )
     ]
-    for load in loads:
-        load.start()
 
     barrier = pltpu.get_barrier_semaphore()
 
@@ -99,6 +103,9 @@
     def _():
         greet(2 * chip + 2)
         greet(2 * chip + 3)
+
+    for load in loads:
+        load.start()
 
     pl.semaphore_wait(barrier, 3 + low.astype(jnp.int32) + high.astype(jnp.int32))
 
@@ -119,10 +126,19 @@
     ring_copy(0, 1, other, nxt).start()
     ring_copy(0, chips - 1, other, prv).start()
 
+    for parity in range(2):
+        pick = (
+            lax.broadcasted_iota(jnp.int32, (width, 2 * width), 1)
+            == 2 * lax.broadcasted_iota(jnp.int32, (width, 2 * width), 0) + parity
+        ).astype(BF16)
+        for f in range(2):
+            for r in range(2):
+                ss[1 + r, parity, f] = dot_t(pick, sc[f, r]).astype(BF16)
+
     fc_up = copy(fc, fs.at[pl.ds(0, 2), 0], h_s.at[0], h_r.at[0], me + 1)
     fc_down = copy(fc, fs.at[pl.ds(0, 2), 2], h_s.at[1], h_r.at[1], me - 1)
-    sc_up = copy(sc.at[1], ss.at[0, :, pl.ds(0, 2)], h_s.at[2], h_r.at[2], me + 1)
-    sc_down = copy(sc.at[0], ss.at[3, :, pl.ds(0, 2)], h_s.at[3], h_r.at[3], me - 1)
+    sc_up = copy(ss.at[2, :, pl.ds(0, 2)], ss.at[0, :, pl.ds(0, 2)], h_s.at[2], h_r.at[2], me + 1)
+    sc_down = copy(ss.at[1, :, pl.ds(0, 2)], ss.at[3, :, pl.ds(0, 2)], h_s.at[3], h_r.at[3], me - 1)
 
     @pl.when(jnp.logical_not(last))
     def _():
@@ -135,8 +151,6 @@
         sc_down.start()
 
     fs[0:2, 1] = fc[...]
-    ss[1, :, 0:2] = sc[0]
-    ss[2, :, 0:2] = sc[1]
 
     @pl.when(first)
     def _():
@@ -150,6 +164,8 @@
         ss[3, :, 0:2] = jnp.zeros((2, 2, width, chan2), BF16)
         bo[2] = jnp.zeros((2, width, chan), BF16)
 
+    loads[0].wait()
+    loads[1].wait()
     own = ring[0].reshape(2 * width, chan)
     queries = dot(own, wq[...]).astype(BF16)
     queries = (dot_t(queries, wk[...]) * (1.0 / math.sqrt(chan))).astype(BF16)
@@ -204,34 +220,39 @@
         fc_down.wait_recv()
         sc_down.wait_recv()
 
-    for load in loads:
+    for load in loads[2:]:
         load.wait()
 
-    def first_conv(times):
-        totals = [None] * 3
-        for a in times:
-            for b in range(3):
-                rows = fs[a : a + 2, b].reshape(2 * width, chan)
-                for c in range(3):
-                    term = dot(rows, w1[a, b, c])
-                    totals[c] = term if totals[c] is None else totals[c] + term
-        return totals
-
-    def second_conv(times, k):
+    def first_conv(a, t, c):
+        frames = len(t)
+        sums = None
+        for b in range(3):
+            rows = fs[a + t[0] : a + t[0] + frames, b].reshape(frames * width, chan)
+            term = dot(rows, w1[a, b, c])
+            sums = term if sums is None else sums + term
+        return sums
+
+    def second_conv(a, t, k):
         taps = (((0, 1), (1, 2)), ((0, 0), (1, 1)), ((1, 0),), ((0, 2),))[k]
+        frames = len(t)
         sums = None
-        for a in times:
-            for b in range(3):
-                for parity, c in taps:
-                    rows = ss[b : b + 2, parity, a : a + 2].reshape(4 * width, chan2)
-                    term = dot(rows, w2[a, b, c])
-                    sums = term if sums is None else sums + term
-        return sums
-
-    for c, part in enumerate(first_conv((0,))):
-        c1[c] = part
+        for b in range(3):
+            for parity, c in taps:
+                rows = ss[b : b + 2, parity, a + t[0] : a + t[0] + frames]
+                term = dot(rows.reshape(2 * frames * width, chan2), w2[a, b, c])
+                sums = term if sums is None else sums + term
+        return sums.reshape(2, frames, width, chan2)
+
+    both = (0, 1)
+    for c in range(3):
+        c1[c] = first_conv(0, both, c)
+        c1[c, :width] += first_conv(1, (0,), c)
     for k in range(4):
-        c2[k] = second_conv((0,), k)
+        c2[k] = second_conv(0, both, k)
+        c2[k, :, 0:1] += second_conv(1, (0,), k)
+    for b in range(3):
+        for c in range(3):
+            wu[b, c] = wu_turned[b, c].T
 
     ring_copy(half, half, 0, nxt).wait_recv()
     ring_copy(half, half, 1, prv).wait_recv()
@@ -283,7 +304,9 @@
                 fs.at[2 + f, 1], fs.at[2 + f, 2], e1_s.at[3], e1_r.at[2 + f], 2 * chip + 2 + f
             ).wait_recv()
 
-    sums = [c1[c] + part for c, part in enumerate(first_conv((1, 2)))]
+    for c in range(3):
+        c1[c, width:] += first_conv(1, (1,), c)
+    sums = [c1[c] + first_conv(2, both, c) for c in range(3)]
     block = from_left(sums[0], width) + sums[1] + from_right(sums[2], width)
     block = block.reshape(2, width, chan)
     bo[1, core] = (mx[core].astype(F32) + jnp.where(core == 0, block[0], block[1])).astype(BF16)
@@ -330,11 +353,27 @@
                 entering = jnp.where(last, 0.0, entering)
             ss[u, parity, 2:4] = entering.astype(BF16).reshape(2, width, chan2)
 
-    late = (1, 2)
-    even = c2[0] + second_conv(late, 0) + from_left(c2[2] + second_conv(late, 2), width)
-    out[:, 0] = (up[:, 0].astype(F32) + even.reshape(2, 2, width, chan2)).astype(BF16)
-    odd = c2[1] + second_conv(late, 1) + from_right(c2[3] + second_conv(late, 3), width)
-    out[:, 1] = (up[:, 1].astype(F32) + odd.reshape(2, 2, width, chan2)).astype(BF16)
+    for k in range(4):
+        c2[k, :, 1:2] += second_conv(1, (1,), k)
+
+    def final(k):
+        return (c2[k] + second_conv(2, both, k)).reshape(4 * width, chan2)
+
+    even = final(0) + from_left(final(2), width)
+    odd = final(1) + from_right(final(3), width)
+    even, odd = (
+        (up[:, parity].astype(F32) + value.reshape(2, 2, width, chan2)).astype(BF16)
+        for parity, value in enumerate((even, odd))
+    )
+    at = lax.broadcasted_iota(jnp.int32, (2 * width, 2 * width), 0)
+    column = lax.broadcasted_iota(jnp.int32, (2 * width, 2 * width), 1)
+    place_at = (column == jnp.where(at < width, 2 * at, 2 * at - 2 * width + 1)).astype(BF16)
+    for f in range(2):
+        for r in range(2):
+            pair = jnp.concatenate([even[r, f], odd[r, f]], axis=0)
+            out[f, r] = lax.dot_general(
+                pair, place_at, (((0,), (0,)), ((), ())), preferred_element_type=F32
+            ).astype(BF16)
 
     swap.wait_send()
     for slot in range(1, chips):
@@ -366,14 +405,15 @@
     chips = n // 2
     feat = features.reshape(2, width, chan)
     fc = first_cache.reshape(2, width, chan)
-    sc = second_cache.reshape(2, 2, width, 2, chan2).transpose(1, 3, 0, 2, 4)
+    sc = second_cache.transpose(0, 1, 3, 2)
+    wu = wu.transpose(0, 1, 3, 2)
     vmem = pl.BlockSpec(memory_space=pltpu.VMEM)
     hbm = pl.BlockSpec(memory_space=pl.ANY)
     dma = pltpu.SemaphoreType.DMA
     out = pl.pallas_call(
         functools.partial(kernel, n),
-        out_shape=jax.ShapeDtypeStruct((2, 2, 2, width, chan2), BF16),
-        in_specs=[vmem] * 7 + [hbm] * 3,
+        out_shape=jax.ShapeDtypeStruct((2, 2, chan2, 2 * width), BF16),
+        in_specs=[vmem] * 3 + [hbm] * 7,
         out_specs=vmem,
         scratch_shapes=[
             pltpu.VMEM((2, width, chan), BF16),
@@ -387,11 +427,16 @@
             pltpu.VMEM((4, 2, 4, width, chan2), BF16),
             pltpu.VMEM((2, 2, 2, width, chan2), BF16),
             pltpu.VMEM((3, 2 * width, chan), F32),
-            pltpu.VMEM((4, 4 * width, chan2), F32),
+            pltpu.VMEM((4, 2, 2, width, chan2), F32),
+            pltpu.VMEM((chan, chan), BF16),
+            pltpu.VMEM((chan, chan), BF16),
+            pltpu.VMEM((chan, chan), BF16),
+            pltpu.VMEM((chan, chan), BF16),
             pltpu.VMEM(w1.shape, BF16),
+            pltpu.VMEM((3, 3, chan, chan2), BF16),
+            pltpu.VMEM(w2.shape, BF16),
             pltpu.VMEM(wu.shape, BF16),
-            pltpu.VMEM(w2.shape, BF16),
-            dma((3,)),
+            dma((7,)),
             dma((1,)),
             dma((1,)),
             dma((chips, 2)),
@@ -408,7 +453,7 @@
         ),
         name="decoder_window",
     )(feat, fc, sc, wq, wk, wv, wo, w1, wu, w2)
-    return out.transpose(2, 0, 3, 1, 4).reshape(2, 2, 2 * width, chan2)
+    return out.transpose(0, 1, 3, 2)
 
 
 def solution(mesh):

time: 60.1 us -> 53.4 us (0.89)
  the two profiles are of different devices: /device:TPU:9 before, /device:TPU:19 now
where the time goes in v2:
time: 53.4 us; the launch traced here: 53.3 us
  Pallas kernels  51.5 us (96%)
  local copies, waits for them, and re-layouts  1.77 us (3%)
    pallas_call x1, Pallas kernels, per_device(): pl.pallas_call(functools.partial(kernel, n), out_shape=jax.ShapeDtypeStru...  51.5 us
    unnamed x1, local copies, waits for them, and re-layouts  1.77 us

profile of v2, /device:TPU:19, one launch (start us, length us, event | category | flops | bytes accessed | tf_op | source)
XLA Modules:
  0.0 53.3 jit_solution(17881047288414168338)
XLA Ops:
  0.0 51.5 %decoder_window.1 = bf16[2,2,192,256]{3,2,1,0:T(8,128)(2,1)} custom-call(bf16[2,128,384]{2,1,0:T(8,128)(2,1)} %bitcast.8, bf16[2,128,384]{2,1,0:T(8,128)(2,1)} %bitcast.9, bf16[2,2,192,256]{3,2,1,0:T(8,128)(2,1)} %bitcast.7, bf16[384,384]{1,0:T(8,128)(2,1)} %wq_hbm.1, bf16[384,384]{1,0:T(8,128)(2,1)} %wk_hbm.1, bf16[384,384]{1,0:T(8,128)(2,1)} %wv_hbm.1, ...), custom_call_target="tpu_custom_call" | custom-call | tf_op jit(solution)/shard_map/decoder_window/pallas_call | solution.py:413
  51.5 1.8 %copy.12 = bf16[2,2,256,192]{2,3,1,0:T(8,128)(2,1)} copy(bf16[2,2,256,192]{2,3,1,0:T(8,128)(2,1)} %bitcast.5) | data formatting | bytes 786432

commit v3 on v2

--- a/solution.py
+++ b/solution.py
@@ -41,7 +41,7 @@
 def kernel(
     n,
     feat, fc, sc, wq_hbm, wk_hbm, wv_hbm, wo_hbm, w1_hbm, wu_hbm, w2_hbm,
-    out,
+    out_0, out_1,
     fb, ring, acc, top, total, fs, mx, bo, ss, up, c1, c2,
     wq, wk, wv, wo, w1, wu, w2, wu_turned,
     l_sem, e0_s, e0_r, g_s, g_r, h_s, h_r, e1_s, e1_r, e2_s, e2_r,
@@ -139,16 +139,6 @@
     fc_down = copy(fc, fs.at[pl.ds(0, 2), 2], h_s.at[1], h_r.at[1], me - 1)
     sc_up = copy(ss.at[2, :, pl.ds(0, 2)], ss.at[0, :, pl.ds(0, 2)], h_s.at[2], h_r.at[2], me + 1)
     sc_down = copy(ss.at[1, :, pl.ds(0, 2)], ss.at[3, :, pl.ds(0, 2)], h_s.at[3], h_r.at[3], me - 1)
-
-    @pl.when(jnp.logical_not(last))
-    def _():
-        fc_up.start()
-        sc_up.start()
-
-    @pl.when(jnp.logical_not(first))
-    def _():
-        fc_down.start()
-        sc_down.start()
 
     fs[0:2, 1] = fc[...]
 
@@ -210,46 +200,43 @@
                 pl.when(row == 1)(ring_copy(chips - step, chips - step - 1, 1, prv).start)
         attend((step, chips - step))
 
-    @pl.when(jnp.logical_not(first))
-    def _():
-        fc_up.wait_recv()
-        sc_up.wait_recv()
-
-    @pl.when(jnp.logical_not(last))
-    def _():
-        fc_down.wait_recv()
-        sc_down.wait_recv()
+    pl.when(jnp.logical_not(last))(fc_up.start)
+    pl.when(jnp.logical_not(first))(fc_down.start)
 
     for load in loads[2:]:
         load.wait()
 
-    def first_conv(a, t, c):
+    def first_conv(a, t, c, taps):
         frames = len(t)
         sums = None
-        for b in range(3):
+        for b in taps:
             rows = fs[a + t[0] : a + t[0] + frames, b].reshape(frames * width, chan)
             term = dot(rows, w1[a, b, c])
             sums = term if sums is None else sums + term
         return sums
 
-    def second_conv(a, t, k):
-        taps = (((0, 1), (1, 2)), ((0, 0), (1, 1)), ((1, 0),), ((0, 2),))[k]
+    def second_conv(a, t, k, taps, at=0, count=2):
+        pairs = (((0, 1), (1, 2)), ((0, 0), (1, 1)), ((1, 0),), ((0, 2),))[k]
         frames = len(t)
         sums = None
-        for b in range(3):
-            for parity, c in taps:
-                rows = ss[b : b + 2, parity, a + t[0] : a + t[0] + frames]
-                term = dot(rows.reshape(2 * frames * width, chan2), w2[a, b, c])
+        for b in taps:
+            for parity, c in pairs:
+                rows = ss[at + b : at + b + count, parity, a + t[0] : a + t[0] + frames]
+                term = dot(rows.reshape(count * frames * width, chan2), w2[a, b, c])
                 sums = term if sums is None else sums + term
-        return sums.reshape(2, frames, width, chan2)
+        return sums.reshape(count, frames, width, chan2)
 
     both = (0, 1)
     for c in range(3):
-        c1[c] = first_conv(0, both, c)
-        c1[c, :width] += first_conv(1, (0,), c)
+        c1[c] = first_conv(0, both, c, (1,))
+        c1[c, :width] += first_conv(1, (0,), c, (1,))
     for k in range(4):
-        c2[k] = second_conv(0, both, k)
-        c2[k, :, 0:1] += second_conv(1, (0,), k)
+        c2[k] = second_conv(0, both, k, (1,))
+        c2[k, 0:1] += second_conv(0, both, k, (2,), 0, 1)
+        c2[k, 1:2] += second_conv(0, both, k, (0,), 1, 1)
+        c2[k, :, 0:1] += second_conv(1, (0,), k, (1,))
+        c2[k, 0:1, 0:1] += second_conv(1, (0,), k, (2,), 0, 1)
+        c2[k, 1:2, 0:1] += second_conv(1, (0,), k, (0,), 1, 1)
     for b in range(3):
         for c in range(3):
             wu[b, c] = wu_turned[b, c].T
@@ -282,6 +269,14 @@
     pl.when(low)(row_down.start)
     to_partner.start()
     mix_partner.start()
+    pl.when(jnp.logical_not(last))(sc_up.start)
+    pl.when(jnp.logical_not(first))(sc_down.start)
+
+    pl.when(jnp.logical_not(first))(fc_up.wait_recv)
+    pl.when(jnp.logical_not(last))(fc_down.wait_recv)
+    for c in range(3):
+        c1[c] += first_conv(0, both, c, (0, 2))
+        c1[c, :width] += first_conv(1, (0,), c, (0, 2))
 
     theirs = 2 + other
     copy(
@@ -305,8 +300,8 @@
             ).wait_recv()
 
     for c in range(3):
-        c1[c, width:] += first_conv(1, (1,), c)
-    sums = [c1[c] + first_conv(2, both, c) for c in range(3)]
+        c1[c, width:] += first_conv(1, (1,), c, (0, 1, 2))
+    sums = [c1[c] + first_conv(2, both, c, (0, 1, 2)) for c in range(3)]
     block = from_left(sums[0], width) + sums[1] + from_right(sums[2], width)
     block = block.reshape(2, width, chan)
     bo[1, core] = (mx[core].astype(F32) + jnp.where(core == 0, block[0], block[1])).astype(BF16)
@@ -325,6 +320,14 @@
         [y[0][c] + y[1][c] for c in range(3)],
         [y[0][c] for c in range(3)],
     ]
+    pl.when(jnp.logical_not(first))(sc_up.wait_recv)
+    pl.when(jnp.logical_not(last))(sc_down.wait_recv)
+    for k in range(4):
+        c2[k, 0:1] += second_conv(0, both, k, (0,), 0, 1)
+        c2[k, 1:2] += second_conv(0, both, k, (2,), 1, 1)
+        c2[k, 0:1, 0:1] += second_conv(1, (0,), k, (0,), 0, 1)
+        c2[k, 1:2, 0:1] += second_conv(1, (0,), k, (2,), 1, 1)
+
     pl.when(jnp.logical_not(first))(bo_up.wait_recv)
     pl.when(jnp.logical_not(last))(bo_down.wait_recv)
     above = bo[0].reshape(2 * width, chan)
@@ -354,10 +357,10 @@
             ss[u, parity, 2:4] = entering.astype(BF16).reshape(2, width, chan2)
 
     for k in range(4):
-        c2[k, :, 1:2] += second_conv(1, (1,), k)
+        c2[k, :, 1:2] += second_conv(1, (1,), k, (0, 1, 2))
 
     def final(k):
-        return (c2[k] + second_conv(2, both, k)).reshape(4 * width, chan2)
+        return (c2[k] + second_conv(2, both, k, (0, 1, 2))).reshape(4 * width, chan2)
 
     even = final(0) + from_left(final(2), width)
     odd = final(1) + from_right(final(3), width)
@@ -368,10 +371,10 @@
     at = lax.broadcasted_iota(jnp.int32, (2 * width, 2 * width), 0)
     column = lax.broadcasted_iota(jnp.int32, (2 * width, 2 * width), 1)
     place_at = (column == jnp.where(at < width, 2 * at, 2 * at - 2 * width + 1)).astype(BF16)
-    for f in range(2):
+    for f, out in enumerate((out_0, out_1)):
         for r in range(2):
             pair = jnp.concatenate([even[r, f], odd[r, f]], axis=0)
-            out[f, r] = lax.dot_general(
+            out[0, r] = lax.dot_general(
                 pair, place_at, (((0,), (0,)), ((), ())), preferred_element_type=F32
             ).astype(BF16)
 
@@ -412,9 +415,9 @@
     dma = pltpu.SemaphoreType.DMA
     out = pl.pallas_call(
         functools.partial(kernel, n),
-        out_shape=jax.ShapeDtypeStruct((2, 2, chan2, 2 * width), BF16),
+        out_shape=[jax.ShapeDtypeStruct((1, 2, chan2, 2 * width), BF16)] * 2,
         in_specs=[vmem] * 3 + [hbm] * 7,
-        out_specs=vmem,
+        out_specs=[vmem] * 2,
         scratch_shapes=[
             pltpu.VMEM((2, width, chan), BF16),
             pltpu.VMEM((chips, 2, width, chan), BF16),
@@ -453,7 +456,7 @@
         ),
         name="decoder_window",
     )(feat, fc, sc, wq, wk, wv, wo, w1, wu, w2)
-    return out.transpose(0, 1, 3, 2)
+    return jnp.concatenate(out, axis=0).transpose(0, 1, 3, 2)
 
 
 def solution(mesh):

time: 53.4 us -> 47.9 us (0.90)
  the two profiles are of different devices: /device:TPU:19 before, /device:TPU:1 now
where the time goes in v3:
time: 47.9 us; the launch traced here: 47.8 us
  Pallas kernels  46 us (96%)
  other arithmetic  1.81 us (4%)
    pallas_call x1, Pallas kernels, per_device(): pl.pallas_call(functools.partial(kernel, n), out_shape=[jax.ShapeDtypeStr...  46 us
    transpose x1, other arithmetic, per_device(): return jnp.concatenate(out, axis=0).transpose(0, 1, 3, 2)  1.81 us

profile of v3, /device:TPU:1, one launch (start us, length us, event | category | flops | bytes accessed | tf_op | source)
XLA Modules:
  0.0 47.8 jit_solution(17559083269754080588)
XLA Ops:
  0.0 46.0 %decoder_window.1 = (bf16[1,2,192,256]{3,2,1,0:T(8,128)(2,1)}, bf16[1,2,192,256]{3,2,1,0:T(8,128)(2,1)}) custom-call(bf16[2,128,384]{2,1,0:T(8,128)(2,1)} %bitcast.8, bf16[2,128,384]{2,1,0:T(8,128)(2,1)} %bitcast.9, bf16[2,2,192,256]{3,2,1,0:T(8,128)(2,1)} %bitcast.7, bf16[384,384]{1,0:T(8,128)(2,1)} %wq_hbm.1, bf16[384,384]{1,0:T(8,128)(2,1)} %wk_hbm.1, ...), custom_call_target="tpu_custom_call" | custom-call | tf_op jit(solution)/shard_map/decoder_window/pallas_call | solution.py:416
  46.0 1.8 %maximum_bitcast_fusion = bf16[2,2,256,192]{2,3,1,0:T(8,128)(2,1)} fusion(bf16[1,2,192,256]{3,2,1,0:T(8,128)(2,1)} %get-tuple-element.8, bf16[1,2,192,256]{3,2,1,0:T(8,128)(2,1)} %get-tuple-element.7), kind=kLoop, calls=%fused_computation | loop fusion | flops 196608 | bytes 786432 | tf_op jit(solution)/shard_map/transpose | solution.py:459

commit v4 on v3

--- a/solution.py
+++ b/solution.py
@@ -40,10 +40,10 @@
 
 def kernel(
     n,
-    feat, fc, sc, wq_hbm, wk_hbm, wv_hbm, wo_hbm, w1_hbm, wu_hbm, w2_hbm,
+    feat, fc_hbm, sc_hbm, wq_hbm, wk_hbm, wv_hbm, wo_hbm, w1_hbm, wu_hbm, w2_hbm,
     out_0, out_1,
     fb, ring, acc, top, total, fs, mx, bo, ss, up, c1, c2,
-    wq, wk, wv, wo, w1, wu, w2, wu_turned,
+    sc, wq, wk, wv, wo, w1, wu, w2, wu_turned,
     l_sem, e0_s, e0_r, g_s, g_r, h_s, h_r, e1_s, e1_r, e2_s, e2_r,
 ):
     width, chan = feat.shape[1], feat.shape[2]
@@ -77,7 +77,7 @@
         pltpu.make_async_copy(src, dst, l_sem.at[k])
         for k, (src, dst) in enumerate(
             (
-                (wq_hbm, wq), (wk_hbm, wk), (wu_hbm, wu_turned), (w1_hbm, w1),
+                (sc_hbm, sc), (wq_hbm, wq), (wk_hbm, wk), (fc_hbm, fs.at[pl.ds(0, 2), 1]), (wu_hbm, wu_turned), (w1_hbm, w1),
                 (w2_hbm, w2), (wv_hbm, wv), (wo_hbm, wo),
             )
         )
@@ -126,6 +126,7 @@
     ring_copy(0, 1, other, nxt).start()
     ring_copy(0, chips - 1, other, prv).start()
 
+    loads[0].wait()
     for parity in range(2):
         pick = (
             lax.broadcasted_iota(jnp.int32, (width, 2 * width), 1)
@@ -135,27 +136,27 @@
             for r in range(2):
                 ss[1 + r, parity, f] = dot_t(pick, sc[f, r]).astype(BF16)
 
-    fc_up = copy(fc, fs.at[pl.ds(0, 2), 0], h_s.at[0], h_r.at[0], me + 1)
-    fc_down = copy(fc, fs.at[pl.ds(0, 2), 2], h_s.at[1], h_r.at[1], me - 1)
+    fc_up = copy(fs.at[pl.ds(0, 2), 1], fs.at[pl.ds(0, 2), 0], h_s.at[0], h_r.at[0], me + 1)
+    fc_down = copy(fs.at[pl.ds(0, 2), 1], fs.at[pl.ds(0, 2), 2], h_s.at[1], h_r.at[1], me - 1)
     sc_up = copy(ss.at[2, :, pl.ds(0, 2)], ss.at[0, :, pl.ds(0, 2)], h_s.at[2], h_r.at[2], me + 1)
     sc_down = copy(ss.at[1, :, pl.ds(0, 2)], ss.at[3, :, pl.ds(0, 2)], h_s.at[3], h_r.at[3], me - 1)
 
-    fs[0:2, 1] = fc[...]
-
     @pl.when(first)
     def _():
-        fs[:, 0] = jnp.zeros((4, width, chan), BF16)
+        for t in range(4):
+            fs[t, 0] = jnp.zeros((width, chan), BF16)
         ss[0, :, 0:2] = jnp.zeros((2, 2, width, chan2), BF16)
         bo[0] = jnp.zeros((2, width, chan), BF16)
 
     @pl.when(last)
     def _():
-        fs[:, 2] = jnp.zeros((4, width, chan), BF16)
+        for t in range(4):
+            fs[t, 2] = jnp.zeros((width, chan), BF16)
         ss[3, :, 0:2] = jnp.zeros((2, 2, width, chan2), BF16)
         bo[2] = jnp.zeros((2, width, chan), BF16)
 
-    loads[0].wait()
     loads[1].wait()
+    loads[2].wait()
     own = ring[0].reshape(2 * width, chan)
     queries = dot(own, wq[...]).astype(BF16)
     queries = (dot_t(queries, wk[...]) * (1.0 / math.sqrt(chan))).astype(BF16)
@@ -186,6 +187,46 @@
         total[...] = sums
         acc[...] = mixed_in
 
+    def first_conv(a, t, c, taps):
+        frames = len(t)
+        sums = None
+        for b in taps:
+            rows = fs[a + t[0] : a + t[0] + frames, b].reshape(frames * width, chan)
+            term = dot(rows, w1[a, b, c])
+            sums = term if sums is None else sums + term
+        return sums
+
+    def second_conv(a, t, k, taps, at=0, count=2):
+        pairs = (((0, 1), (1, 2)), ((0, 0), (1, 1)), ((1, 0),), ((0, 2),))[k]
+        frames = len(t)
+        sums = None
+        for b in taps:
+            for parity, c in pairs:
+                rows = ss[at + b : at + b + count, parity, a + t[0] : a + t[0] + frames]
+                term = dot(rows.reshape(count * frames * width, chan2), w2[a, b, c])
+                sums = term if sums is None else sums + term
+        return sums.reshape(count, frames, width, chan2)
+
+    both = (0, 1)
+
+    def early(step):
+        if step == 1:
+            for load in loads[3:]:
+                load.wait()
+            for b in range(3):
+                for c in range(3):
+                    wu[b, c] = wu_turned[b, c].T
+            for c in range(3):
+                c1[c] = first_conv(0, both, c, (1,))
+                c1[c, :width] += first_conv(1, (0,), c, (1,))
+        for k in {2: (0, 1), 3: (2, 3)}.get(min(step, 4), ()):
+            c2[k] = second_conv(0, both, k, (1,))
+            c2[k, 0:1] += second_conv(0, both, k, (2,), 0, 1)
+            c2[k, 1:2] += second_conv(0, both, k, (0,), 1, 1)
+            c2[k, :, 0:1] += second_conv(1, (0,), k, (1,))
+            c2[k, 0:1, 0:1] += second_conv(1, (0,), k, (2,), 0, 1)
+            c2[k, 1:2, 0:1] += second_conv(1, (0,), k, (0,), 1, 1)
+
     for step in range(1, half):
         for row in (core, other):
             ring_copy(step, step, row, nxt).wait_recv()
@@ -198,48 +239,11 @@
                 ring_copy(chips - step, chips - step - 1, row, prv).start()
             else:
                 pl.when(row == 1)(ring_copy(chips - step, chips - step - 1, 1, prv).start)
+        if step + 1 == half:
+            pl.when(jnp.logical_not(last))(fc_up.start)
+            pl.when(jnp.logical_not(first))(fc_down.start)
         attend((step, chips - step))
-
-    pl.when(jnp.logical_not(last))(fc_up.start)
-    pl.when(jnp.logical_not(first))(fc_down.start)
-
-    for load in loads[2:]:
-        load.wait()
-
-    def first_conv(a, t, c, taps):
-        frames = len(t)
-        sums = None
-        for b in taps:
-            rows = fs[a + t[0] : a + t[0] + frames, b].reshape(frames * width, chan)
-            term = dot(rows, w1[a, b, c])
-            sums = term if sums is None else sums + term
-        return sums
-
-    def second_conv(a, t, k, taps, at=0, count=2):
-        pairs = (((0, 1), (1, 2)), ((0, 0), (1, 1)), ((1, 0),), ((0, 2),))[k]
-        frames = len(t)
-        sums = None
-        for b in taps:
-            for parity, c in pairs:
-                rows = ss[at + b : at + b + count, parity, a + t[0] : a + t[0] + frames]
-                term = dot(rows.reshape(count * frames * width, chan2), w2[a, b, c])
-                sums = term if sums is None else sums + term
-        return sums.reshape(count, frames, width, chan2)
-
-    both = (0, 1)
-    for c in range(3):
-        c1[c] = first_conv(0, both, c, (1,))
-        c1[c, :width] += first_conv(1, (0,), c, (1,))
-    for k in range(4):
-        c2[k] = second_conv(0, both, k, (1,))
-        c2[k, 0:1] += second_conv(0, both, k, (2,), 0, 1)
-        c2[k, 1:2] += second_conv(0, both, k, (0,), 1, 1)
-        c2[k, :, 0:1] += second_conv(1, (0,), k, (1,))
-        c2[k, 0:1, 0:1] += second_conv(1, (0,), k, (2,), 0, 1)
-        c2[k, 1:2, 0:1] += second_conv(1, (0,), k, (0,), 1, 1)
-    for b in range(3):
-        for c in range(3):
-            wu[b, c] = wu_turned[b, c].T
+        early(step)
 
     ring_copy(half, half, 0, nxt).wait_recv()
     ring_copy(half, half, 1, prv).wait_recv()
@@ -298,6 +302,7 @@
             copy(
                 fs.at[2 + f, 1], fs.at[2 + f, 2], e1_s.at[3], e1_r.at[2 + f], 2 * chip + 2 + f
             ).wait_recv()
+
 
     for c in range(3):
         c1[c, width:] += first_conv(1, (1,), c, (0, 1, 2))
@@ -416,7 +421,7 @@
     out = pl.pallas_call(
         functools.partial(kernel, n),
         out_shape=[jax.ShapeDtypeStruct((1, 2, chan2, 2 * width), BF16)] * 2,
-        in_specs=[vmem] * 3 + [hbm] * 7,
+        in_specs=[vmem] + [hbm] * 9,
         out_specs=[vmem] * 2,
         scratch_shapes=[
             pltpu.VMEM((2, width, chan), BF16),
@@ -431,6 +436,7 @@
             pltpu.VMEM((2, 2, 2, width, chan2), BF16),
             pltpu.VMEM((3, 2 * width, chan), F32),
             pltpu.VMEM((4, 2, 2, width, chan2), F32),
+            pltpu.VMEM(sc.shape, BF16),
             pltpu.VMEM((chan, chan), BF16),
             pltpu.VMEM((chan, chan), BF16),
             pltpu.VMEM((chan, chan), BF16),
@@ -439,7 +445,7 @@
             pltpu.VMEM((3, 3, chan, chan2), BF16),
             pltpu.VMEM(w2.shape, BF16),
             pltpu.VMEM(wu.shape, BF16),
-            dma((7,)),
+            dma((9,)),
             dma((1,)),
             dma((1,)),
             dma((chips, 2)),

time: 47.9 us -> 47.6 us (level)
  no operation moved by 1% of the time
where the time goes in v4:
time: 47.6 us; the launch traced here: 47.4 us
  Pallas kernels  45.6 us (96%)
  other arithmetic  1.81 us (4%)
    pallas_call x1, Pallas kernels, per_device(): pl.pallas_call(functools.partial(kernel, n), out_shape=[jax.ShapeDtypeStr...  45.6 us
    transpose x1, other arithmetic, per_device(): return jnp.concatenate(out, axis=0).transpose(0, 1, 3, 2)  1.81 us

profile of v4, /device:TPU:1, one launch (start us, length us, event | category | flops | bytes accessed | tf_op | source)
XLA Modules:
  0.0 47.4 jit_solution(15971456703651774832)
XLA Ops:
  0.0 45.6 %decoder_window.1 = (bf16[1,2,192,256]{3,2,1,0:T(8,128)(2,1)}, bf16[1,2,192,256]{3,2,1,0:T(8,128)(2,1)}) custom-call(bf16[2,128,384]{2,1,0:T(8,128)(2,1)} %bitcast.8, bf16[2,128,384]{2,1,0:T(8,128)(2,1)} %bitcast.9, bf16[2,2,192,256]{3,2,1,0:T(8,128)(2,1)} %bitcast.7, bf16[384,384]{1,0:T(8,128)(2,1)} %wq_hbm.1, bf16[384,384]{1,0:T(8,128)(2,1)} %wk_hbm.1, ...), custom_call_target="tpu_custom_call" | custom-call | tf_op jit(solution)/shard_map/decoder_window/pallas_call | solution.py:421
  45.6 1.8 %maximum_bitcast_fusion = bf16[2,2,256,192]{2,3,1,0:T(8,128)(2,1)} fusion(bf16[1,2,192,256]{3,2,1,0:T(8,128)(2,1)} %get-tuple-element.8, bf16[1,2,192,256]{3,2,1,0:T(8,128)(2,1)} %get-tuple-element.7), kind=kLoop, calls=%fused_computation | loop fusion | flops 196608 | bytes 786432 | tf_op jit(solution)/shard_map/transpose | solution.py:465
